TPU v7x, 32 devices: a whole 2x2x4 slice. The times are simulated.
32 devices in a mesh: dp: 8 (over z, y), tensor: 4 (over x, core).
Axes of the slice: x: 2, y: 2, z: 4, core: 2. Of those that a mesh axis runs over, the one named last changes fastest.
Arguments:
- gate_act: bfloat16 [2048, 14336], P('dp', 'tensor'), may hold values from -6 to 6
- up_act: bfloat16 [2048, 14336], P('dp', 'tensor'), may hold values from -6 to 6
- out_grad: bfloat16 [2048, 4096], P(('dp', 'tensor')), may hold values from -6 to 6
- down_weight: bfloat16 [4096, 14336], P(None, 'tensor'), may hold values from -0.046875 to 0.046875
- master_weight: float32 [4096, 14336], P('dp', 'tensor'), may hold values from -0.046875 to 0.046875
- round_bits: int32 [4096, 14336], P('dp', 'tensor'), may hold values from 0 to 16383
Outputs:
- layer_out: bfloat16 [2048, 4096], P(('dp', 'tensor'))
- gate_grad: bfloat16 [2048, 14336], P('dp', 'tensor')
- up_grad: bfloat16 [2048, 14336], P('dp', 'tensor')
- new_master: float32 [4096, 14336], P('dp', 'tensor')
- new_weight: bfloat16 [4096, 14336], P('dp', 'tensor')
All inputs are finite; a program needn't handle non-finite values.
Results may differ from a plain program's by a relative error of at most 0.0012.
The roundings to bfloat16 on the way count: a program that leaves them out, or rounds other values in their place, can miss the bound.
Values may be sent and summed in bfloat16 or wider, within the bound.
A program may use at most 128 MiB of HBM per device.

v0:
```python
import jax
import jax.numpy as jnp
from jax import lax
from jax.sharding import PartitionSpec as P

learn_rate = 0.5
dither_scale = 1.0 / 64.0


def local(gate_act, up_act, out_grad, down_weight, master_weight, round_bits):
    g = gate_act.astype(jnp.float32)
    u = up_act.astype(jnp.float32)
    sig = jax.nn.sigmoid(g)
    act = g * sig
    hidden = (act * u).astype(jnp.bfloat16)
    layer_out = lax.psum_scatter(
        lax.dot_general(
            hidden, down_weight, (((1,), (1,)), ((), ())), preferred_element_type=jnp.float32
        ),
        "tensor",
        scatter_dimension=0,
        tiled=True,
    ).astype(jnp.bfloat16)
    grad_full = lax.all_gather(out_grad, "tensor", axis=0, tiled=True)
    hidden_grad = jnp.dot(grad_full, down_weight, preferred_element_type=jnp.float32)
    up_grad = (hidden_grad * act).astype(jnp.bfloat16)
    gate_grad = (hidden_grad * u * sig * (1.0 + g * (1.0 - sig))).astype(jnp.bfloat16)
    grad_cols = lax.all_to_all(grad_full, "dp", split_axis=1, concat_axis=0, tiled=True)
    weight_grad = lax.dot_general(
        grad_cols,
        lax.all_gather(hidden, "dp", axis=0, tiled=True),
        (((0,), (0,)), ((), ())),
        preferred_element_type=jnp.float32,
    )
    tokens_all = hidden.shape[0] * lax.axis_size("dp")
    new_master = master_weight - learn_rate * (weight_grad / tokens_all)
    dither = (round_bits.astype(jnp.float32) + 0.5) / 16384.0
    new_weight = (new_master + (dither - 0.5) * jnp.abs(new_master) * dither_scale).astype(
        jnp.bfloat16
    )
    return (layer_out, gate_grad, up_grad, new_master, new_weight)


def solution(mesh):
    return jax.shard_map(
        local,
        mesh=mesh,
        in_specs=(
            P("dp", "tensor"),
            P("dp", "tensor"),
            P(("dp", "tensor"), None),
            P(None, "tensor"),
            P("dp", "tensor"),
            P("dp", "tensor"),
        ),
        out_specs=(
            P(("dp", "tensor"), None),
            P("dp", "tensor"),
            P("dp", "tensor"),
            P("dp", "tensor"),
            P("dp", "tensor"),
        ),
        check_vma=False,
    )
```

profile of v0, /device:TPU:0, one launch (start us, length us, event | category | flops | bytes accessed | tf_op | source)
XLA Modules:
  0.0 357.7 jit_solution(15139885616963474572)
XLA Ops:
  7.2 0.0 all-gather.3.cloned.1.call-start
  7.2 0.7 all-gather.3.cloned.1.call-update
  7.9 0.0 reduce-scatter.2.cloned.1.call-start
  7.9 26.9 %all-gather.3.cloned.1.call-done = bf16[256,4096]{1,0:T(8,128)(2,1)} async-done(((bf16[64,4096]{1,0:T(8,128)(2,1)}), bf16[256,4096]{1,0:T(8,128)(2,1)}) %all-gather.3.cloned.1.call-update) | async-done | bytes 2097168 | tf_op jit(solution)/shard_map/all_gather | solution.py:24
  34.9 16.9 %multiply_convert_fusion = (bf16[256,3584]{1,0:T(8,128)(2,1)}, bf16[256,3584]{1,0:T(8,128)(2,1)}, bf16[256,3584]{1,0:T(8,128)(2,1)S(1)}) fusion(bf16[256,3584]{1,0:T(8,128)(2,1)} %param.6, bf16[256,3584]{1,0:T(8,128)(2,1)} %param.7, bf16[256,4096]{1,0:T(8,128)(2,1)} %all-gather.3.cloned.1.call-done, bf16[4096,3584]{1,0:T(8,128)(2,1)} %param.9), kind=kOutput, calls=%fused_computation.15 | convolution fusion | flops 7531790336 | bytes 40632320 | tf_op jit(solution)/shard_map/dot_general | solution.py:25
  51.8 0.0 copy-start.1
  51.8 1.2 copy-done.1
  53.0 15.6 %fusion.8 = f32[256,4096]{1,0:T(8,128)} fusion(bf16[256,3584]{1,0:T(8,128)(2,1)S(1)} %get-tuple-element.27, bf16[4096,3584]{1,0:T(8,128)(2,1)} %param.9), kind=kOutput, calls=%fused_computation.16 | convolution fusion | flops 7516192768 | bytes 35389440 | tf_op jit(solution)/shard_map/dot_general | solution.py:17
  68.6 0.0 copy-start
  68.6 0.0 reduce-scatter.2.cloned.1.call-update
  68.6 0.0 all-gather.5.cloned.1.call-start
  68.7 0.7 all-gather.5.cloned.1.call-update
  69.4 0.8 copy-done
  70.2 2.4 copy.25
  72.6 5.5 %all-to-all-start = ((bf16[256,8,512]{0,2,1:T(8,128)(2,1)}), bf16[256,8,512]{0,2,1:T(8,128)(2,1)S(1)}, u32[]{:S(2)}, u32[]{:S(2)}) async-start(bf16[256,8,512]{0,2,1:T(8,128)(2,1)} %bitcast.12), calls=%async_computation.1 | async-start | bytes 4194304 | tf_op jit(solution)/shard_map/all_to_all | solution.py:28
  78.1 8.5 %copy.27 = f32[512,3584]{0,1:T(8,128)} copy(f32[512,3584]{1,0:T(8,128)} %param.10) | data formatting | bytes 14680064 | tf_op args[4]
  86.6 8.8 %copy.28 = s32[512,3584]{0,1:T(8,128)} copy(s32[512,3584]{1,0:T(8,128)} %param.11) | data formatting | bytes 14680064 | tf_op args[5]
  95.5 31.3 %all-to-all-done = bf16[256,8,512]{0,2,1:T(8,128)(2,1)S(1)} async-done(((bf16[256,8,512]{0,2,1:T(8,128)(2,1)}), bf16[256,8,512]{0,2,1:T(8,128)(2,1)S(1)}, u32[]{:S(2)}, u32[]{:S(2)}) %all-to-all-start) | async-done | bytes 2097184 | tf_op jit(solution)/shard_map/all_to_all | solution.py:28
  126.8 2.4 copy.26
  129.2 2.1 convert_element_type.27
  131.2 186.5 %all-gather.5.cloned.1.call-done = bf16[2048,3584]{1,0:T(8,128)(2,1)} async-done(((bf16[256,3584]{1,0:T(8,128)(2,1)}), bf16[2048,3584]{1,0:T(8,128)(2,1)}) %all-gather.5.cloned.1.call-update) | async-done | bytes 14680080 | tf_op jit(solution)/shard_map/all_gather | solution.py:31
  317.8 19.1 %add_convert_fusion = (bf16[512,3584]{0,1:T(8,128)(2,1)}, f32[512,3584]{0,1:T(8,128)}) fusion(s32[512,3584]{0,1:T(8,128)} %copy.28, f32[512,3584]{0,1:T(8,128)} %copy.27, bf16[2048,3584]{1,0:T(8,128)(2,1)} %all-gather.5.cloned.1.call-done, bf16[2048,512]{1,0:T(8,128)(2,1)} %bitcast.13), kind=kOutput, calls=%fused_computation.1 | convolution fusion | flops 7536377856 | bytes 42467328 | tf_op jit(solution)/shard_map/dot_general | solution.py:29
  336.9 5.9 %copy.30 = bf16[512,3584]{1,0:T(8,128)(2,1)} copy(bf16[512,3584]{0,1:T(8,128)(2,1)} %get-tuple-element.28) | data formatting | bytes 7340032
  342.8 8.4 %copy.29 = f32[512,3584]{1,0:T(8,128)} copy(f32[512,3584]{0,1:T(8,128)} %get-tuple-element.29) | data formatting | bytes 14680064
  (1 shorter events, 0.0 us)
Async XLA Ops:
  7.2 27.7 %all-gather.3.cloned.1.call-start = ((), (), s32[]{:S(2)}) async-start(), calls=%async_computation.3 | async-start | bytes 2621440 | tf_op jit(solution)/shard_map/all_gather | solution.py:24
  7.9 121.3 %reduce-scatter.2.cloned.1.call-start = ((), (), s32[]{:S(2)}) async-start(), calls=%async_computation.2 | async-start | bytes 5242880 | tf_op jit(solution)/shard_map/reduce_scatter | solution.py:16
  51.8 1.2 copy-start.1
  68.6 1.6 copy-start
  68.6 249.1 %all-gather.5.cloned.1.call-start = ((), (), s32[]{:S(2)}) async-start(), calls=%async_computation.4 | async-start | bytes 16515072 | tf_op jit(solution)/shard_map/all_gather | solution.py:31
  72.6 54.2 %all-to-all-start = ((bf16[256,8,512]{0,2,1:T(8,128)(2,1)}), bf16[256,8,512]{0,2,1:T(8,128)(2,1)S(1)}, u32[]{:S(2)}, u32[]{:S(2)}) async-start(bf16[256,8,512]{0,2,1:T(8,128)(2,1)} %bitcast.12), calls=%async_computation.1 | async-start | bytes 4194304 | tf_op jit(solution)/shard_map/all_to_all | solution.py:28
Sparse Core Ops, SparseCore 0:
  9.6 25.2 all-gather.2
  68.7 44.4 reduce-scatter.1
  115.7 202.0 all-gather.4
where the time goes:
time: 358 us
  waiting for transfers between devices  246 us (69%)
  matrix products  51.6 us (14%)
  local copies, waits for them, and re-layouts  38.5 us (11%)
  between operations  13.8 us (4%)
  starting transfers between devices  5.63 us (2%)
    all_gather x1, waiting for transfers between devices, local(): lax.all_gather(hidden, 'dp', axis=0, tiled=True)  187 us
    unnamed x8, local copies, waits for them, and re-layouts  33.6 us
    all_to_all x1, waiting for transfers between devices, local(): lax.all_to_all(grad_full, 'dp', split_axis=1, concat_axis=0, tiled=True)  31.3 us
    all_gather x1, waiting for transfers between devices, local(): grad_full = lax.all_gather(out_grad, 'tensor', axis=0, tiled=True)  26.9 us
    dot_general x1, matrix products, local(): lax.dot_general(grad_cols, lax.all_gather(hidden, 'dp', axis=0, tiled=Tru...  19.1 us
    dot_general x1, matrix products, local(): jnp.dot(grad_full, down_weight, preferred_element_type=jnp.float32)  16.9 us
    dot_general x1, matrix products, local(): lax.dot_general(hidden, down_weight, (((1,), (1,)), ((), ())), preferred_...  15.6 us
  transfers between devices with their start and end apart: 4, of which 3 were waited for; matrix products, arithmetic and copies ran while one was open for 7% of the time, Pallas kernels for 0%

commit v1 on v0

v1 whole, which is shorter than its diff:
```python
import functools

import jax
import jax.numpy as jnp
from jax import lax
from jax.experimental import pallas as pl
from jax.experimental.pallas import tpu as pltpu
from jax.sharding import PartitionSpec as P

learn_rate = 0.5
dither_scale = 1.0 / 64.0


def arrivals(lines):
    return [
        [
            (way, hops)
            for hops in range(1, lines)
            for way, good in ((1, z >= hops), (-1, z + hops < lines))
            if good
        ]
        for z in range(lines)
    ]


def gradient_sum(place, grad_ref, blocks, first):
    total = None
    for i, block in enumerate(blocks):
        part = jnp.dot(grad_ref[place[first + i]], block[...], preferred_element_type=jnp.float32)
        total = part if total is None else total + part
    return total


def early_kernel(count, tokens_all, place, grad_ref, *refs):
    master_ref, out_ref = refs[count:]
    total = gradient_sum(place, grad_ref, refs[:count], 0)
    out_ref[...] = master_ref[...] - learn_rate * (total / tokens_all)


def final_kernel(first, tokens_all, place, grad_ref, block, master_ref, bits_ref, new_master_ref, new_weight_ref):
    total = gradient_sum(place, grad_ref, [block], first)
    new_master = master_ref[...] - learn_rate * (total / tokens_all)
    new_master_ref[...] = new_master
    dither = (bits_ref[...].astype(jnp.float32) + 0.5) / 16384.0
    new_weight_ref[...] = (
        new_master + (dither - 0.5) * jnp.abs(new_master) * dither_scale
    ).astype(jnp.bfloat16)


def update(place, grads, blocks, master, bits, first, tokens_all):
    rows, columns = master.shape
    depth = blocks[0].shape[0]
    tile = 256 if columns % 256 == 0 else 128
    whole = pl.BlockSpec(grads.shape, lambda j, place: (0, 0, 0))
    wide = pl.BlockSpec((rows, tile), lambda j, place: (0, j))
    block = pl.BlockSpec((depth, tile), lambda j, place: (0, j))
    last = bits is not None
    new_master = jax.ShapeDtypeStruct(master.shape, jnp.float32)
    new_weight = jax.ShapeDtypeStruct(master.shape, jnp.bfloat16)
    return pl.pallas_call(
        functools.partial(final_kernel, first, tokens_all)
        if last
        else functools.partial(early_kernel, len(blocks), tokens_all),
        grid_spec=pltpu.PrefetchScalarGridSpec(
            num_scalar_prefetch=1,
            grid=(columns // tile,),
            in_specs=[whole] + [block] * len(blocks) + [wide] * (2 if last else 1),
            out_specs=[wide, wide] if last else wide,
        ),
        out_shape=[new_master, new_weight] if last else new_master,
        compiler_params=pltpu.CompilerParams(vmem_limit_bytes=40 * 2**20),
        cost_estimate=pl.CostEstimate(
            flops=2 * rows * columns * depth * len(blocks),
            bytes_accessed=rows * columns * (14 if last else 8) + len(blocks) * depth * columns * 2,
            transcendentals=0,
        ),
    )(place, grads, *blocks, master, *([bits] if last else []))


def local(gate_act, up_act, out_grad, down_weight, master_weight, round_bits):
    n = lax.axis_size("dp")
    t = lax.axis_size("tensor")
    lines = n // 2
    me = lax.axis_index("dp")
    z, y = me // 2, me % 2
    order = arrivals(lines)
    came = {}

    def hop(rising, falling, step):
        rising = lax.ppermute(
            rising, "dp", [(2 * i + j, 2 * i + 2 + j) for i in range(step - 1, lines - 1) for j in range(2)]
        )
        falling = lax.ppermute(
            falling, "dp", [(2 * i + j, 2 * i - 2 + j) for i in range(1, lines - step + 1) for j in range(2)]
        )
        return rising, falling

    def arrived(k):
        block = None
        for key in sorted({order[i][k] for i in range(lines)}):
            here = functools.reduce(jnp.logical_or, [z == i for i in range(lines) if order[i][k] == key])
            block = came[key] if block is None else jnp.where(here, came[key], block)
        return block

    def swap(block):
        return lax.ppermute(block, "dp", [(2 * i + j, 2 * i + 1 - j) for i in range(lines) for j in range(2)])

    g = gate_act.astype(jnp.float32)
    u = up_act.astype(jnp.float32)
    sig = jax.nn.sigmoid(g)
    act = g * sig
    hidden = (act * u).astype(jnp.bfloat16)
    grad_full = lax.all_gather(out_grad, "tensor", axis=0, tiled=True)
    rising, falling = hop(hidden, hidden, 1)
    cross = [swap(hidden)]
    hidden, out_grad = lax.optimization_barrier((hidden, out_grad))
    own_cols = lax.all_to_all(out_grad, "dp", split_axis=1, concat_axis=0, tiled=True)
    partial = lax.dot_general(
        hidden, down_weight, (((1,), (1,)), ((), ())), preferred_element_type=jnp.float32
    )
    rising, falling, cross[0], partial, grad_full, own_cols = lax.optimization_barrier(
        (rising, falling, cross[0], partial, grad_full, own_cols)
    )
    layer_out = lax.psum_scatter(partial, "tensor", scatter_dimension=0, tiled=True).astype(jnp.bfloat16)
    hidden_grad = jnp.dot(grad_full, down_weight, preferred_element_type=jnp.float32)
    up_grad = (hidden_grad * act).astype(jnp.bfloat16)
    gate_grad = (hidden_grad * u * sig * (1.0 + g * (1.0 - sig))).astype(jnp.bfloat16)
    along = []
    for step in range(1, lines):
        came[1, step], came[-1, step] = rising, falling
        if step < lines - 1:
            rising, falling = hop(rising, falling, step + 1)
        along.append(arrived(step - 1))
        cross.append(swap(along[-1]))
        if step == 1:
            rising, falling, cross[1], up_grad, gate_grad = lax.optimization_barrier(
                (rising, falling, cross[1], up_grad, gate_grad)
            )
            cols = lax.all_gather(own_cols, "tensor", axis=0, tiled=False)
            rows = cols.shape[-1]
            grads = cols.reshape(t, n, out_grad.shape[0], rows).transpose(1, 3, 0, 2).reshape(n, rows, -1)
        elif step == lines - 2:
            rising, falling, cross[step], grads = lax.optimization_barrier(
                (rising, falling, cross[step], grads)
            )
        elif step < lines - 1:
            rising, falling, cross[step] = lax.optimization_barrier((rising, falling, cross[step]))
    owner = [z]
    for k in range(lines - 1):
        shift = sum(jnp.where(z == i, order[i][k][0] * order[i][k][1], 0) for i in range(lines))
        owner.append(z - shift)
    place = jnp.stack([2 * o + y for o in owner] + [2 * o + 1 - y for o in owner]).astype(jnp.int32)
    tokens_all = hidden.shape[0] * n
    master = update(place, grads, [hidden] + along + cross[:-1], master_weight, None, 0, tokens_all)
    new_master, new_weight = update(place, grads, cross[-1:], master, round_bits, n - 1, tokens_all)
    return (layer_out, gate_grad, up_grad, new_master, new_weight)


def solution(mesh):
    return jax.shard_map(
        local,
        mesh=mesh,
        in_specs=(
            P("dp", "tensor"),
            P("dp", "tensor"),
            P(("dp", "tensor"), None),
            P(None, "tensor"),
            P("dp", "tensor"),
            P("dp", "tensor"),
        ),
        out_specs=(
            P(("dp", "tensor"), None),
            P("dp", "tensor"),
            P("dp", "tensor"),
            P("dp", "tensor"),
            P("dp", "tensor"),
        ),
        check_vma=False,
    )
```

time: 358 us -> 229 us (0.64)
  waiting for transfers between devices: 246 us -> 97.5 us
  Pallas kernels: 0 us -> 32.6 us
  local copies, waits for them, and re-layouts: 38.5 us -> 16.7 us
  matrix products: 51.6 us -> 32.5 us
  starting transfers between devices: 5.63 us -> 23.8 us
  other arithmetic: 2.07 us -> 10.7 us
    all_gather x1, waiting for transfers between devices: 187 us -> 0.02 us  [local(): cols = lax.all_gather(own_cols, 'tensor', axis=0, tiled=False)]
    ppermute x0 -> x10, waiting for transfers between devices: none -> 68.3 us  [the longest x4 64.2 us: swap(): lax.ppermute(block, 'dp', [(2 * i + j, 2 * i + 1 - j) for i in range(line...]
    pallas_call x0 -> x2, Pallas kernels: none -> 32.6 us  [update(): pl.pallas_call(functools.partial(final_kernel, first, tokens_all) if last...]
    all_gather x1, waiting for transfers between devices: 26.9 us -> 0.02 us  [local(): grad_full = lax.all_gather(out_grad, 'tensor', axis=0, tiled=True)]
    unnamed x8 -> x20, local copies, waits for them, and re-layouts: 33.6 us -> 8.71 us
    ppermute x0 -> x10, starting transfers between devices: none -> 19.8 us  [the longest x3 9.67 us: hop(): lax.ppermute(rising, 'dp', [(2 * i + j, 2 * i + 2 + j) for i in range(ste...]
    dot_general x1 -> x0, matrix products: 19.1 us -> none  [local(): lax.dot_general(grad_cols, lax.all_gather(hidden, 'dp', axis=0, tiled=Tru...]
    select_n x0 -> x3, other arithmetic: none -> 5.43 us  [arrived(): block = came[key] if block is None else jnp.where(here, came[key], block)]
  transfers between devices with their start and end apart: 4 -> 14, of which waited for: 3 -> 5; matrix products, arithmetic and copies ran while one was open for 7% -> 22% of each run, Pallas kernels for 0% -> 14%
where the time goes in v1:
time: 229 us; the launch traced here: 228 us
  waiting for transfers between devices  97.5 us (43%)
  Pallas kernels  32.6 us (14%)
  matrix products  32.5 us (14%)
  starting transfers between devices  23.8 us (10%)
  local copies, waits for them, and re-layouts  16.7 us (7%)
  between operations  13.9 us (6%)
  other arithmetic  10.7 us (5%)
    ppermute x4, waiting for transfers between devices, swap(): lax.ppermute(block, 'dp', [(2 * i + j, 2 * i + 1 - j) for i in range(line...  64.2 us
    pallas_call x2, Pallas kernels, update(): pl.pallas_call(functools.partial(final_kernel, first, tokens_all) if last...  32.6 us
    all_to_all x1, waiting for transfers between devices, local(): lax.all_to_all(out_grad, 'dp', split_axis=1, concat_axis=0, tiled=True)  28.5 us
    dot_general x1, matrix products, local(): jnp.dot(grad_full, down_weight, preferred_element_type=jnp.float32)  17.2 us
    dot_general x1, matrix products, local(): lax.dot_general(hidden, down_weight, (((1,), (1,)), ((), ())), preferred_...  15.2 us
    ppermute x3, starting transfers between devices, hop(): lax.ppermute(rising, 'dp', [(2 * i + j, 2 * i + 2 + j) for i in range(ste...  9.67 us
    unnamed x20, local copies, waits for them, and re-layouts  8.71 us
    ppermute x4, starting transfers between devices, swap(): lax.ppermute(block, 'dp', [(2 * i + j, 2 * i + 1 - j) for i in range(line...  6.33 us
  transfers between devices with their start and end apart: 14, of which 5 were waited for; matrix products, arithmetic and copies ran while one was open for 22% of the time, Pallas kernels for 14%

profile of v1, /device:TPU:0, one launch (start us, length us, event | category | flops | bytes accessed | tf_op | source)
XLA Modules:
  0.0 227.7 jit_solution(13467941748965077358)
XLA Ops:
  7.9 3.2 %fusion.refs_0_ = bf16[256,3584]{1,0:T(8,128)(2,1)S(1)} fusion(bf16[256,3584]{1,0:T(8,128)(2,1)} %param.7, bf16[256,3584]{1,0:T(8,128)(2,1)} %param.6), kind=kLoop, calls=%fused_computation.5 | loop fusion | flops 7340032 | bytes 5505024 | tf_op jit(solution)/shard_map/convert_element_type | solution.py:112
  11.1 3.0 %collective-permute-start.2 = (bf16[256,3584]{1,0:T(8,128)(2,1)S(1)}, bf16[256,3584]{1,0:T(8,128)(2,1)}, u32[]{:S(2)}, u32[]{:S(2)}) collective-permute-start(bf16[256,3584]{1,0:T(8,128)(2,1)S(1)} %fusion.refs_0_), channel_id=1, source_target_pairs={{0,4},{4,0},{8,12},{12,8},{16,20},{20,16},{24,28},{28,24},{1,5},{5... | collective-permute-start | bytes 5505032 | tf_op jit(solution)/shard_map/ppermute | solution.py:106
  15.4 5.8 %collective-permute-start = (bf16[256,3584]{1,0:T(8,128)(2,1)S(1)}, bf16[256,3584]{1,0:T(8,128)(2,1)}, u32[]{:S(2)}, u32[]{:S(2)}) collective-permute-start(bf16[256,3584]{1,0:T(8,128)(2,1)S(1)} %fusion.refs_0_), channel_id=1, source_target_pairs={{0,8},{4,12},{8,16},{12,20},{16,24},{20,28},{1,9},{5,13},{9,17},{1... | collective-permute-start | bytes 5505032 | tf_op jit(solution)/shard_map/ppermute | solution.py:90
  22.1 3.9 %all-to-all-start = ((bf16[64,8,512]{2,0,1:T(8,128)(2,1)}), bf16[64,8,512]{2,0,1:T(8,128)(2,1)S(1)}, u32[]{:S(2)}, u32[]{:S(2)}) async-start(bf16[64,8,512]{2,0,1:T(8,128)(2,1)} %bitcast.22), calls=%async_computation | async-start | bytes 1048576 | tf_op jit(solution)/shard_map/all_to_all | solution.py:117
  26.0 15.2 %fusion.8 = f32[256,4096]{1,0:T(8,128)} fusion(bf16[256,3584]{1,0:T(8,128)(2,1)S(1)} %fusion.refs_0_, bf16[4096,3584]{1,0:T(8,128)(2,1)} %param.9), kind=kOutput, calls=%fused_computation.18 | convolution fusion | flops 7516192768 | bytes 35389440 | tf_op jit(solution)/shard_map/dot_general | solution.py:118
  41.2 28.5 %all-to-all-done = bf16[64,8,512]{2,0,1:T(8,128)(2,1)S(1)} async-done(((bf16[64,8,512]{2,0,1:T(8,128)(2,1)}), bf16[64,8,512]{2,0,1:T(8,128)(2,1)S(1)}, u32[]{:S(2)}, u32[]{:S(2)}) %all-to-all-start) | async-done | bytes 524320 | tf_op jit(solution)/shard_map/all_to_all | solution.py:117
  70.7 1.9 collective-permute-start.3
  73.9 1.7 broadcast_select_fusion.refs_1_
  76.8 17.2 %fusion.3 = (bf16[256,3584]{1,0:T(8,128)(2,1)}, bf16[256,3584]{1,0:T(8,128)(2,1)}) fusion(bf16[256,3584]{1,0:T(8,128)(2,1)} %param.7, bf16[256,3584]{1,0:T(8,128)(2,1)} %param.6, bf16[256,4096]{1,0:T(8,128)(2,1)} %all-gather.4.cloned.1.call-done, bf16[4096,3584]{1,0:T(8,128)(2,1)} %param.9), kind=kOutput, calls=%fused_computation.8 | convolution fusion | flops 7529955328 | bytes 38797312 | tf_op jit(solution)/shard_map/dot_general | solution.py:125
  94.1 22.0 %collective-permute-done.5.refs_5_ = bf16[256,3584]{1,0:T(8,128)(2,1)} collective-permute-done((bf16[256,3584]{1,0:T(8,128)(2,1)S(1)}, bf16[256,3584]{1,0:T(8,128)(2,1)}, u32[]{:S(2)}, u32[]{:S(2)}) %collective-permute-start.5) | collective-permute-done | bytes 1835040 | tf_op jit(solution)/shard_map/ppermute | solution.py:106
  116.1 1.9 select_select_fusion.1.refs_2_
  118.7 1.9 collective-permute-start.6
  121.9 3.1 %copy.19 = bf16[8,512,4,64]{1,3,2,0:T(8,128)(2,1)} copy(bf16[8,512,4,64]{1,3,0,2:T(8,128)(2,1)} %bitcast.24) | data formatting | bytes 4194304 | tf_op jit(solution)/shard_map/transpose | solution.py:141
  125.0 32.3 %collective-permute-done.8.refs_6_ = bf16[256,3584]{1,0:T(8,128)(2,1)} collective-permute-done((bf16[256,3584]{1,0:T(8,128)(2,1)S(1)}, bf16[256,3584]{1,0:T(8,128)(2,1)}, u32[]{:S(2)}, u32[]{:S(2)}) %collective-permute-start.8) | collective-permute-done | bytes 1835040 | tf_op jit(solution)/shard_map/ppermute | solution.py:106
  157.3 4.0 %collective-permute-done.7 = bf16[256,3584]{1,0:T(8,128)(2,1)} collective-permute-done((bf16[256,3584]{1,0:T(8,128)(2,1)}, bf16[256,3584]{1,0:T(8,128)(2,1)}, u32[]{:S(2)}, u32[]{:S(2)}) %collective-permute-start.7) | collective-permute-done | bytes 1835040 | tf_op jit(solution)/shard_map/ppermute | solution.py:93
  161.4 1.8 select_select_fusion.refs_3_
  163.2 1.8 collective-permute-start.9
  165.1 3.9 %copy.21.grad_ref = bf16[8,512,256]{2,1,0:T(8,128)(2,1)} copy(bf16[8,512,256]{1,2,0:T(8,128)(2,1)} %bitcast.23) | data formatting | bytes 4194304 | tf_op jit(solution)/shard_map/optimization_barrier | solution.py:143
  169.0 1.5 copy-done.3
  173.5 17.3 %shard_map.101.master_ref = f32[512,3584]{1,0:T(8,128)} custom-call(s32[8]{0:T(128)S(1)} %stack.35.place, bf16[8,512,256]{2,1,0:T(8,128)(2,1)} %copy.21.grad_ref, bf16[256,3584]{1,0:T(8,128)(2,1)S(1)} %copy-done.5, bf16[256,3584]{1,0:T(8,128)(2,1)S(1)} %copy-done.3, bf16[256,3584]{1,0:T(8,128)(2,1)S(1)} %copy-done.7, ...), custom_call_target="tpu_custom_call" | custom-call | flops 6576668672 | bytes 27525120 | tf_op jit(solution)/shard_map/pallas_call | solution.py:60
  190.8 9.9 %collective-permute-done.9.block = bf16[256,3584]{1,0:T(8,128)(2,1)} collective-permute-done((bf16[256,3584]{1,0:T(8,128)(2,1)S(1)}, bf16[256,3584]{1,0:T(8,128)(2,1)}, u32[]{:S(2)}, u32[]{:S(2)}) %collective-permute-start.9) | collective-permute-done | bytes 1835040 | tf_op jit(solution)/shard_map/ppermute | solution.py:106
  200.7 3.1 %copy-done = f32[512,3584]{1,0:T(8,128)S(1)} copy-done((f32[512,3584]{1,0:T(8,128)S(1)}, f32[512,3584]{1,0:T(8,128)}, u32[]{:S(2)}) %copy-start) | copy-done | bytes 7340056
  203.8 15.3 %shard_map.102 = (f32[512,3584]{1,0:T(8,128)}, bf16[512,3584]{1,0:T(8,128)(2,1)}) custom-call(s32[8]{0:T(128)S(1)} %stack.35.place, bf16[8,512,256]{2,1,0:T(8,128)(2,1)S(1)} %copy-done.1, bf16[256,3584]{1,0:T(8,128)(2,1)} %collective-permute-done.9.block, f32[512,3584]{1,0:T(8,128)S(1)} %copy-done, s32[512,3584]{1,0:T(8,128)} %bits_ref.1), custom_call_target="tpu_custom_call" | custom-call | flops 939524096 | bytes 27525120 | tf_op jit(solution)/shard_map/pallas_call | solution.py:60
  219.1 2.1 convert_element_type.21
  (40 shorter events, 11.3 us)
Async XLA Ops:
  7.2 62.6 %all-gather.4.cloned.1.call-start = ((), (), s32[]{:S(2)}) async-start(), calls=%async_computation.2 | async-start | bytes 2621440 | tf_op jit(solution)/shard_map/all_gather | solution.py:113
  7.9 13.4 %copy-start.8 = (bf16[64,4096]{1,0:T(8,128)(2,1)S(1)}, bf16[64,4096]{1,0:T(8,128)(2,1)}, u32[]{:S(2)}) copy-start(bf16[64,4096]{1,0:T(8,128)(2,1)} %param.8) | copy-start | bytes 1572868
  11.1 30.1 %copy-start.4 = (bf16[256,3584]{1,0:T(8,128)(2,1)}, bf16[256,3584]{1,0:T(8,128)(2,1)S(1)}, u32[]{:S(2)}) copy-start(bf16[256,3584]{1,0:T(8,128)(2,1)S(1)} %fusion.refs_0_) | copy-start | bytes 5505028
  11.1 58.6 %collective-permute-start.2 = (bf16[256,3584]{1,0:T(8,128)(2,1)S(1)}, bf16[256,3584]{1,0:T(8,128)(2,1)}, u32[]{:S(2)}, u32[]{:S(2)}) collective-permute-start(bf16[256,3584]{1,0:T(8,128)(2,1)S(1)} %fusion.refs_0_), channel_id=1, source_target_pairs={{0,4},{4,0},{8,12},{12,8},{16,20},{20,16},{24,28},{28,24},{1,5},{5... | collective-permute-start | bytes 5505032 | tf_op jit(solution)/shard_map/ppermute | solution.py:106
  14.2 55.6 %collective-permute-start.1 = (bf16[256,3584]{1,0:T(8,128)(2,1)S(1)}, bf16[256,3584]{1,0:T(8,128)(2,1)}, u32[]{:S(2)}, u32[]{:S(2)}) collective-permute-start(bf16[256,3584]{1,0:T(8,128)(2,1)S(1)} %fusion.refs_0_), channel_id=1, source_target_pairs={{8,0},{12,4},{16,8},{20,12},{24,16},{28,20},{9,1},{13,5},{17,9},{2... | collective-permute-start | bytes 5505032 | tf_op jit(solution)/shard_map/ppermute | solution.py:93
  15.4 54.3 %collective-permute-start = (bf16[256,3584]{1,0:T(8,128)(2,1)S(1)}, bf16[256,3584]{1,0:T(8,128)(2,1)}, u32[]{:S(2)}, u32[]{:S(2)}) collective-permute-start(bf16[256,3584]{1,0:T(8,128)(2,1)S(1)} %fusion.refs_0_), channel_id=1, source_target_pairs={{0,8},{4,12},{8,16},{12,20},{16,24},{20,28},{1,9},{5,13},{9,17},{1... | collective-permute-start | bytes 5505032 | tf_op jit(solution)/shard_map/ppermute | solution.py:90
  22.1 47.7 %all-to-all-start = ((bf16[64,8,512]{2,0,1:T(8,128)(2,1)}), bf16[64,8,512]{2,0,1:T(8,128)(2,1)S(1)}, u32[]{:S(2)}, u32[]{:S(2)}) async-start(bf16[64,8,512]{2,0,1:T(8,128)(2,1)} %bitcast.22), calls=%async_computation | async-start | bytes 1048576 | tf_op jit(solution)/shard_map/all_to_all | solution.py:117
  26.0 95.9 %all-gather.6.cloned.1.call-start = ((), (), s32[]{:S(2)}) async-start(), calls=%async_computation.4 | async-start | bytes 2621440 | tf_op jit(solution)/shard_map/all_gather | solution.py:139
  69.8 0.8 copy-start.9
  70.6 148.5 %reduce-scatter.2.cloned.1.call-start = ((), (), s32[]{:S(2)}) async-start(), calls=%async_computation.3 | async-start | bytes 5242880 | tf_op jit(solution)/shard_map/reduce_scatter | solution.py:124
  70.7 45.4 %collective-permute-start.3 = (bf16[256,3584]{1,0:T(8,128)(2,1)}, bf16[256,3584]{1,0:T(8,128)(2,1)}, u32[]{:S(2)}, u32[]{:S(2)}) collective-permute-start(bf16[256,3584]{1,0:T(8,128)(2,1)} %collective-permute-done), channel_id=1, source_target_pairs={{8,16},{12,20},{16,24},{20,28},{9,17},{13,21},{17,25},{21,29},{10,... | collective-permute-start | bytes 5505032 | tf_op jit(solution)/shard_map/ppermute | solution.py:90
  72.6 43.5 %collective-permute-start.4 = (bf16[256,3584]{1,0:T(8,128)(2,1)}, bf16[256,3584]{1,0:T(8,128)(2,1)}, u32[]{:S(2)}, u32[]{:S(2)}) collective-permute-start(bf16[256,3584]{1,0:T(8,128)(2,1)} %collective-permute-done.1), channel_id=1, source_target_pairs={{8,0},{12,4},{16,8},{20,12},{9,1},{13,5},{17,9},{21,13},{10,2},{14... | collective-permute-start | bytes 5505032 | tf_op jit(solution)/shard_map/ppermute | solution.py:93
  75.6 1.2 copy-start.2
  75.6 40.4 %collective-permute-start.5 = (bf16[256,3584]{1,0:T(8,128)(2,1)S(1)}, bf16[256,3584]{1,0:T(8,128)(2,1)}, u32[]{:S(2)}, u32[]{:S(2)}) collective-permute-start(bf16[256,3584]{1,0:T(8,128)(2,1)S(1)} %broadcast_select_fusion.refs_1_), channel_id=1, source_target_pairs={{0,4},{4,0},{8,12},{12,8},{16,20},{20,16},{24,28},{28,24},{1,5},{5... | collective-permute-start | bytes 5505032 | tf_op jit(solution)/shard_map/ppermute | solution.py:106
  118.0 7.1 %copy-start.6 = (bf16[256,3584]{1,0:T(8,128)(2,1)}, bf16[256,3584]{1,0:T(8,128)(2,1)S(1)}, u32[]{:S(2)}) copy-start(bf16[256,3584]{1,0:T(8,128)(2,1)S(1)} %select_select_fusion.1.refs_2_) | copy-start | bytes 5505028
  118.0 39.3 %collective-permute-start.8 = (bf16[256,3584]{1,0:T(8,128)(2,1)S(1)}, bf16[256,3584]{1,0:T(8,128)(2,1)}, u32[]{:S(2)}, u32[]{:S(2)}) collective-permute-start(bf16[256,3584]{1,0:T(8,128)(2,1)S(1)} %select_select_fusion.1.refs_2_), channel_id=1, source_target_pairs={{0,4},{4,0},{8,12},{12,8},{16,20},{20,16},{24,28},{28,24},{1,5},{5... | collective-permute-start | bytes 5505032 | tf_op jit(solution)/shard_map/ppermute | solution.py:106
  118.7 38.7 %collective-permute-start.6 = (bf16[256,3584]{1,0:T(8,128)(2,1)}, bf16[256,3584]{1,0:T(8,128)(2,1)}, u32[]{:S(2)}, u32[]{:S(2)}) collective-permute-start(bf16[256,3584]{1,0:T(8,128)(2,1)} %collective-permute-done.3), channel_id=1, source_target_pairs={{16,24},{20,28},{17,25},{21,29},{18,26},{22,30},{19,27},{23,31}} | collective-permute-start | bytes 5505032 | tf_op jit(solution)/shard_map/ppermute | solution.py:90
  120.6 40.8 %collective-permute-start.7 = (bf16[256,3584]{1,0:T(8,128)(2,1)}, bf16[256,3584]{1,0:T(8,128)(2,1)}, u32[]{:S(2)}, u32[]{:S(2)}) collective-permute-start(bf16[256,3584]{1,0:T(8,128)(2,1)} %collective-permute-done.4), channel_id=1, source_target_pairs={{8,0},{12,4},{9,1},{13,5},{10,2},{14,6},{11,3},{15,7}} | collective-permute-start | bytes 5505032 | tf_op jit(solution)/shard_map/ppermute | solution.py:93
  163.2 37.6 %collective-permute-start.9 = (bf16[256,3584]{1,0:T(8,128)(2,1)S(1)}, bf16[256,3584]{1,0:T(8,128)(2,1)}, u32[]{:S(2)}, u32[]{:S(2)}) collective-permute-start(bf16[256,3584]{1,0:T(8,128)(2,1)S(1)} %select_select_fusion.refs_3_), channel_id=1, source_target_pairs={{0,4},{4,0},{8,12},{12,8},{16,20},{20,16},{24,28},{28,24},{1,5},{5... | collective-permute-start | bytes 5505032 | tf_op jit(solution)/shard_map/ppermute | solution.py:106
  169.0 1.5 copy-start.3
  170.5 1.5 copy-start.5
  172.0 1.5 copy-start.7
  173.5 27.2 %copy-start.1 = (bf16[8,512,256]{2,1,0:T(8,128)(2,1)S(1)}, bf16[8,512,256]{2,1,0:T(8,128)(2,1)}, u32[]{:S(2)}) copy-start(bf16[8,512,256]{2,1,0:T(8,128)(2,1)} %copy.21.grad_ref) | copy-start | bytes 6291460
  200.7 3.1 %copy-start = (f32[512,3584]{1,0:T(8,128)S(1)}, f32[512,3584]{1,0:T(8,128)}, u32[]{:S(2)}) copy-start(f32[512,3584]{1,0:T(8,128)} %shard_map.101.master_ref) | copy-start | bytes 22020100
Sparse Core Ops, SparseCore 0:
  9.6 25.2 all-gather.3
  70.7 24.0 all-gather.5
  97.3 44.4 reduce-scatter.1

commit v2 on v1

--- a/solution.py
+++ b/solution.py
@@ -113,15 +113,14 @@
     grad_full = lax.all_gather(out_grad, "tensor", axis=0, tiled=True)
     rising, falling = hop(hidden, hidden, 1)
     cross = [swap(hidden)]
-    hidden, out_grad = lax.optimization_barrier((hidden, out_grad))
-    own_cols = lax.all_to_all(out_grad, "dp", split_axis=1, concat_axis=0, tiled=True)
     partial = lax.dot_general(
         hidden, down_weight, (((1,), (1,)), ((), ())), preferred_element_type=jnp.float32
     )
-    rising, falling, cross[0], partial, grad_full, own_cols = lax.optimization_barrier(
-        (rising, falling, cross[0], partial, grad_full, own_cols)
+    rising, falling, cross[0], partial, grad_full, out_grad = lax.optimization_barrier(
+        (rising, falling, cross[0], partial, grad_full, out_grad)
     )
     layer_out = lax.psum_scatter(partial, "tensor", scatter_dimension=0, tiled=True).astype(jnp.bfloat16)
+    own_cols = lax.all_to_all(out_grad, "dp", split_axis=1, concat_axis=0, tiled=True)
     hidden_grad = jnp.dot(grad_full, down_weight, preferred_element_type=jnp.float32)
     up_grad = (hidden_grad * act).astype(jnp.bfloat16)
     gate_grad = (hidden_grad * u * sig * (1.0 + g * (1.0 - sig))).astype(jnp.bfloat16)
@@ -133,8 +132,8 @@
         along.append(arrived(step - 1))
         cross.append(swap(along[-1]))
         if step == 1:
-            rising, falling, cross[1], up_grad, gate_grad = lax.optimization_barrier(
-                (rising, falling, cross[1], up_grad, gate_grad)
+            rising, falling, cross[1], up_grad, gate_grad, own_cols, layer_out = lax.optimization_barrier(
+                (rising, falling, cross[1], up_grad, gate_grad, own_cols, layer_out)
             )
             cols = lax.all_gather(own_cols, "tensor", axis=0, tiled=False)
             rows = cols.shape[-1]

time: 229 us -> 233 us (1.017)
  starting transfers between devices: 23.8 us -> 28.1 us
    all_to_all x1, waiting for transfers between devices: 28.5 us -> 0.01 us  [local(): lax.all_to_all(out_grad, 'dp', split_axis=1, concat_axis=0, tiled=True)]
    all_gather x1, waiting for transfers between devices: 0.02 us -> 16.9 us  [local(): cols = lax.all_gather(own_cols, 'tensor', axis=0, tiled=False)]
    reduce_scatter x1, waiting for transfers between devices: 0.01 us -> 15.6 us  [local(): lax.psum_scatter(partial, 'tensor', scatter_dimension=0, tiled=True)]
    ppermute x4, waiting for transfers between devices: 64.2 us -> 54.6 us  [swap(): lax.ppermute(block, 'dp', [(2 * i + j, 2 * i + 1 - j) for i in range(line...]
    ppermute x3, waiting for transfers between devices: 4.05 us -> 10.1 us  [hop(): lax.ppermute(falling, 'dp', [(2 * i + j, 2 * i - 2 + j) for i in range(1,...]
    all_to_all x1, starting transfers between devices: 3.87 us -> 7.1 us  [local(): lax.all_to_all(out_grad, 'dp', split_axis=1, concat_axis=0, tiled=True)]
    unnamed x20 -> x24, local copies, waits for them, and re-layouts: 8.71 us -> 7.62 us
  transfers between devices with their start and end apart: 14 -> 14, of which waited for: 5 -> 10; matrix products, arithmetic and copies ran while one was open for 22% -> 21% of each run, Pallas kernels for 14% -> 7%
where the time goes in v2:
time: 233 us; the launch traced here: 231 us
  waiting for transfers between devices  99.1 us (43%)
  Pallas kernels  32.6 us (14%)
  matrix products  31.5 us (14%)
  starting transfers between devices  28.1 us (12%)
  local copies, waits for them, and re-layouts  15.6 us (7%)
  between operations  13.9 us (6%)
  other arithmetic  10.7 us (5%)
    ppermute x4, waiting for transfers between devices, swap(): lax.ppermute(block, 'dp', [(2 * i + j, 2 * i + 1 - j) for i in range(line...  54.6 us
    pallas_call x2, Pallas kernels, update(): pl.pallas_call(functools.partial(final_kernel, first, tokens_all) if last...  32.6 us
    all_gather x1, waiting for transfers between devices, local(): cols = lax.all_gather(own_cols, 'tensor', axis=0, tiled=False)  16.9 us
    dot_general x1, matrix products, local(): jnp.dot(grad_full, down_weight, preferred_element_type=jnp.float32)  16.2 us
    reduce_scatter x1, waiting for transfers between devices, local(): lax.psum_scatter(partial, 'tensor', scatter_dimension=0, tiled=True)  15.6 us
    dot_general x1, matrix products, local(): lax.dot_general(hidden, down_weight, (((1,), (1,)), ((), ())), preferred_...  15.3 us
    ppermute x3, waiting for transfers between devices, hop(): lax.ppermute(falling, 'dp', [(2 * i + j, 2 * i - 2 + j) for i in range(1,...  10.1 us
    ppermute x3, starting transfers between devices, hop(): lax.ppermute(rising, 'dp', [(2 * i + j, 2 * i + 2 + j) for i in range(ste...  9.83 us
  transfers between devices with their start and end apart: 14, of which 10 were waited for; matrix products, arithmetic and copies ran while one was open for 21% of the time, Pallas kernels for 7%

profile of v2, /device:TPU:0, one launch (start us, length us, event | category | flops | bytes accessed | tf_op | source)
XLA Modules:
  0.0 231.4 jit_solution(15467154674221965078)
XLA Ops:
  7.9 3.1 %fusion.refs_0_ = bf16[256,3584]{1,0:T(8,128)(2,1)S(1)} fusion(bf16[256,3584]{1,0:T(8,128)(2,1)} %param.7, bf16[256,3584]{1,0:T(8,128)(2,1)} %param.6), kind=kLoop, calls=%fused_computation.5 | loop fusion | flops 7340032 | bytes 5505024 | tf_op jit(solution)/shard_map/convert_element_type | solution.py:112
  11.1 3.0 %collective-permute-start.2 = (bf16[256,3584]{1,0:T(8,128)(2,1)S(1)}, bf16[256,3584]{1,0:T(8,128)(2,1)}, u32[]{:S(2)}, u32[]{:S(2)}) collective-permute-start(bf16[256,3584]{1,0:T(8,128)(2,1)S(1)} %fusion.refs_0_), channel_id=1, source_target_pairs={{0,4},{4,0},{8,12},{12,8},{16,20},{20,16},{24,28},{28,24},{1,5},{5... | collective-permute-start | bytes 5505032 | tf_op jit(solution)/shard_map/ppermute | solution.py:106
  15.4 5.8 %collective-permute-start = (bf16[256,3584]{1,0:T(8,128)(2,1)S(1)}, bf16[256,3584]{1,0:T(8,128)(2,1)}, u32[]{:S(2)}, u32[]{:S(2)}) collective-permute-start(bf16[256,3584]{1,0:T(8,128)(2,1)S(1)} %fusion.refs_0_), channel_id=1, source_target_pairs={{0,8},{4,12},{8,16},{12,20},{16,24},{20,28},{1,9},{5,13},{9,17},{1... | collective-permute-start | bytes 5505032 | tf_op jit(solution)/shard_map/ppermute | solution.py:90
  21.2 15.3 %fusion.8 = f32[256,4096]{1,0:T(8,128)} fusion(bf16[256,3584]{1,0:T(8,128)(2,1)S(1)} %fusion.refs_0_, bf16[4096,3584]{1,0:T(8,128)(2,1)} %param.9), kind=kOutput, calls=%fused_computation.18 | convolution fusion | flops 7516192768 | bytes 35389440 | tf_op jit(solution)/shard_map/dot_general | solution.py:116
  36.5 17.7 %collective-permute-done.2.refs_4_ = bf16[256,3584]{1,0:T(8,128)(2,1)} collective-permute-done((bf16[256,3584]{1,0:T(8,128)(2,1)S(1)}, bf16[256,3584]{1,0:T(8,128)(2,1)}, u32[]{:S(2)}, u32[]{:S(2)}) %collective-permute-start.2) | collective-permute-done | bytes 1835040 | tf_op jit(solution)/shard_map/ppermute | solution.py:106
  54.3 3.3 %collective-permute-done.1 = bf16[256,3584]{1,0:T(8,128)(2,1)} collective-permute-done((bf16[256,3584]{1,0:T(8,128)(2,1)S(1)}, bf16[256,3584]{1,0:T(8,128)(2,1)}, u32[]{:S(2)}, u32[]{:S(2)}) %collective-permute-start.1) | collective-permute-done | bytes 1835040 | tf_op jit(solution)/shard_map/ppermute | solution.py:93
  59.6 7.1 %all-to-all-start = ((bf16[64,8,512]{2,0,1:T(8,128)(2,1)}), bf16[64,8,512]{2,0,1:T(8,128)(2,1)S(1)}, u32[]{:S(2)}, u32[]{:S(2)}) async-start(bf16[64,8,512]{2,0,1:T(8,128)(2,1)} %bitcast.22), calls=%async_computation | async-start | bytes 1048576 | tf_op jit(solution)/shard_map/all_to_all | solution.py:123
  66.8 2.1 collective-permute-start.3
  70.2 1.9 broadcast_select_fusion.refs_1_
  72.1 1.9 collective-permute-start.5
  74.0 16.2 %fusion.3 = (bf16[256,3584]{1,0:T(8,128)(2,1)}, bf16[256,3584]{1,0:T(8,128)(2,1)}) fusion(bf16[256,3584]{1,0:T(8,128)(2,1)S(1)} %copy-done.10, bf16[256,3584]{1,0:T(8,128)(2,1)S(1)} %copy-done.11, bf16[256,4096]{1,0:T(8,128)(2,1)} %all-gather.4.cloned.1.call-done, bf16[4096,3584]{1,0:T(8,128)(2,1)} %param.9), kind=kOutput, calls=%fused_computation.8 | convolution fusion | flops 7529955328 | bytes 38797312 | tf_op jit(solution)/shard_map/dot_general | solution.py:124
  90.3 15.6 %reduce-scatter.2.cloned.1.call-done = f32[64,4096]{1,0:T(8,128)} async-done(((f32[256,4096]{1,0:T(8,128)}), f32[64,4096]{1,0:T(8,128)}) %reduce-scatter.2.cloned.1.call-update) | async-done | bytes 1048592 | tf_op jit(solution)/shard_map/reduce_scatter | solution.py:122
  105.9 2.1 convert_element_type.23
  108.0 7.0 %collective-permute-done.5.refs_5_ = bf16[256,3584]{1,0:T(8,128)(2,1)} collective-permute-done((bf16[256,3584]{1,0:T(8,128)(2,1)S(1)}, bf16[256,3584]{1,0:T(8,128)(2,1)}, u32[]{:S(2)}, u32[]{:S(2)}) %collective-permute-start.5) | collective-permute-done | bytes 1835040 | tf_op jit(solution)/shard_map/ppermute | solution.py:106
  120.0 1.9 collective-permute-start.6
  123.2 16.9 %all-gather.6.cloned.1.call-done = bf16[2048,512]{1,0:T(8,128)(2,1)} async-done(((bf16[512,512]{1,0:T(8,128)(2,1)}), bf16[2048,512]{1,0:T(8,128)(2,1)}) %all-gather.6.cloned.1.call-update) | async-done | bytes 2097168 | tf_op jit(solution)/shard_map/all_gather | solution.py:138
  140.1 3.1 %copy.19 = bf16[8,512,4,64]{1,3,2,0:T(8,128)(2,1)} copy(bf16[8,512,4,64]{1,3,0,2:T(8,128)(2,1)} %bitcast.24) | data formatting | bytes 4194304 | tf_op jit(solution)/shard_map/transpose | solution.py:140
  143.2 16.3 %collective-permute-done.8.refs_6_ = bf16[256,3584]{1,0:T(8,128)(2,1)} collective-permute-done((bf16[256,3584]{1,0:T(8,128)(2,1)S(1)}, bf16[256,3584]{1,0:T(8,128)(2,1)}, u32[]{:S(2)}, u32[]{:S(2)}) %collective-permute-start.8) | collective-permute-done | bytes 1835040 | tf_op jit(solution)/shard_map/ppermute | solution.py:106
  159.5 5.4 %collective-permute-done.7 = bf16[256,3584]{1,0:T(8,128)(2,1)} collective-permute-done((bf16[256,3584]{1,0:T(8,128)(2,1)}, bf16[256,3584]{1,0:T(8,128)(2,1)}, u32[]{:S(2)}, u32[]{:S(2)}) %collective-permute-start.7) | collective-permute-done | bytes 1835040 | tf_op jit(solution)/shard_map/ppermute | solution.py:93
  167.2 3.9 %copy.21.grad_ref = bf16[8,512,256]{2,1,0:T(8,128)(2,1)} copy(bf16[8,512,256]{1,2,0:T(8,128)(2,1)} %bitcast.23) | data formatting | bytes 4194304 | tf_op jit(solution)/shard_map/optimization_barrier | solution.py:142
  175.6 17.3 %shard_map.101.master_ref = f32[512,3584]{1,0:T(8,128)} custom-call(s32[8]{0:T(128)S(1)} %stack.35.place, bf16[8,512,256]{2,1,0:T(8,128)(2,1)} %copy.21.grad_ref, bf16[256,3584]{1,0:T(8,128)(2,1)S(1)} %copy-done.5, bf16[256,3584]{1,0:T(8,128)(2,1)S(1)} %copy-done.3, bf16[256,3584]{1,0:T(8,128)(2,1)S(1)} %copy-done.7, ...), custom_call_target="tpu_custom_call" | custom-call | flops 6576668672 | bytes 27525120 | tf_op jit(solution)/shard_map/pallas_call | solution.py:60
  193.0 13.5 %collective-permute-done.9.block = bf16[256,3584]{1,0:T(8,128)(2,1)} collective-permute-done((bf16[256,3584]{1,0:T(8,128)(2,1)S(1)}, bf16[256,3584]{1,0:T(8,128)(2,1)}, u32[]{:S(2)}, u32[]{:S(2)}) %collective-permute-start.9) | collective-permute-done | bytes 1835040 | tf_op jit(solution)/shard_map/ppermute | solution.py:106
  206.5 3.1 %copy-done = f32[512,3584]{1,0:T(8,128)S(1)} copy-done((f32[512,3584]{1,0:T(8,128)S(1)}, f32[512,3584]{1,0:T(8,128)}, u32[]{:S(2)}) %copy-start) | copy-done | bytes 7340056
  209.6 15.3 %shard_map.102 = (f32[512,3584]{1,0:T(8,128)}, bf16[512,3584]{1,0:T(8,128)(2,1)}) custom-call(s32[8]{0:T(128)S(1)} %stack.35.place, bf16[8,512,256]{2,1,0:T(8,128)(2,1)S(1)} %copy-done.1, bf16[256,3584]{1,0:T(8,128)(2,1)} %collective-permute-done.9.block, f32[512,3584]{1,0:T(8,128)S(1)} %copy-done, s32[512,3584]{1,0:T(8,128)} %bits_ref.1), custom_call_target="tpu_custom_call" | custom-call | flops 939524096 | bytes 27525120 | tf_op jit(solution)/shard_map/pallas_call | solution.py:60
  (44 shorter events, 18.4 us)
Async XLA Ops:
  7.2 51.5 %all-gather.4.cloned.1.call-start = ((), (), s32[]{:S(2)}) async-start(), calls=%async_computation.2 | async-start | bytes 2621440 | tf_op jit(solution)/shard_map/all_gather | solution.py:113
  7.9 98.0 %reduce-scatter.2.cloned.1.call-start = ((), (), s32[]{:S(2)}) async-start(), calls=%async_computation.3 | async-start | bytes 5242880 | tf_op jit(solution)/shard_map/reduce_scatter | solution.py:122
  11.1 25.4 %copy-start.4 = (bf16[256,3584]{1,0:T(8,128)(2,1)}, bf16[256,3584]{1,0:T(8,128)(2,1)S(1)}, u32[]{:S(2)}) copy-start(bf16[256,3584]{1,0:T(8,128)(2,1)S(1)} %fusion.refs_0_) | copy-start | bytes 5505028
  11.1 43.2 %collective-permute-start.2 = (bf16[256,3584]{1,0:T(8,128)(2,1)S(1)}, bf16[256,3584]{1,0:T(8,128)(2,1)}, u32[]{:S(2)}, u32[]{:S(2)}) collective-permute-start(bf16[256,3584]{1,0:T(8,128)(2,1)S(1)} %fusion.refs_0_), channel_id=1, source_target_pairs={{0,4},{4,0},{8,12},{12,8},{16,20},{20,16},{24,28},{28,24},{1,5},{5... | collective-permute-start | bytes 5505032 | tf_op jit(solution)/shard_map/ppermute | solution.py:106
  14.1 43.5 %collective-permute-start.1 = (bf16[256,3584]{1,0:T(8,128)(2,1)S(1)}, bf16[256,3584]{1,0:T(8,128)(2,1)}, u32[]{:S(2)}, u32[]{:S(2)}) collective-permute-start(bf16[256,3584]{1,0:T(8,128)(2,1)S(1)} %fusion.refs_0_), channel_id=1, source_target_pairs={{8,0},{12,4},{16,8},{20,12},{24,16},{28,20},{9,1},{13,5},{17,9},{2... | collective-permute-start | bytes 5505032 | tf_op jit(solution)/shard_map/ppermute | solution.py:93
  15.4 43.2 %collective-permute-start = (bf16[256,3584]{1,0:T(8,128)(2,1)S(1)}, bf16[256,3584]{1,0:T(8,128)(2,1)}, u32[]{:S(2)}, u32[]{:S(2)}) collective-permute-start(bf16[256,3584]{1,0:T(8,128)(2,1)S(1)} %fusion.refs_0_), channel_id=1, source_target_pairs={{0,8},{4,12},{8,16},{12,20},{16,24},{20,28},{1,9},{5,13},{9,17},{1... | collective-permute-start | bytes 5505032 | tf_op jit(solution)/shard_map/ppermute | solution.py:90
  36.5 22.2 %copy-start.8 = (bf16[64,4096]{1,0:T(8,128)(2,1)S(1)}, bf16[64,4096]{1,0:T(8,128)(2,1)}, u32[]{:S(2)}) copy-start(bf16[64,4096]{1,0:T(8,128)(2,1)} %param.8) | copy-start | bytes 1572868
  59.6 48.4 %all-to-all-start = ((bf16[64,8,512]{2,0,1:T(8,128)(2,1)}), bf16[64,8,512]{2,0,1:T(8,128)(2,1)S(1)}, u32[]{:S(2)}, u32[]{:S(2)}) async-start(bf16[64,8,512]{2,0,1:T(8,128)(2,1)} %bitcast.22), calls=%async_computation | async-start | bytes 1048576 | tf_op jit(solution)/shard_map/all_to_all | solution.py:123
  66.7 73.4 %all-gather.6.cloned.1.call-start = ((), (), s32[]{:S(2)}) async-start(), calls=%async_computation.4 | async-start | bytes 2621440 | tf_op jit(solution)/shard_map/all_gather | solution.py:138
  66.7 7.3 %copy-start.10 = (bf16[256,3584]{1,0:T(8,128)(2,1)S(1)}, bf16[256,3584]{1,0:T(8,128)(2,1)}, u32[]{:S(2)}) copy-start(bf16[256,3584]{1,0:T(8,128)(2,1)} %param.7) | copy-start | bytes 5505028
  66.7 7.3 %copy-start.11 = (bf16[256,3584]{1,0:T(8,128)(2,1)S(1)}, bf16[256,3584]{1,0:T(8,128)(2,1)}, u32[]{:S(2)}) copy-start(bf16[256,3584]{1,0:T(8,128)(2,1)} %param.6) | copy-start | bytes 5505028
  66.8 48.2 %collective-permute-start.3 = (bf16[256,3584]{1,0:T(8,128)(2,1)}, bf16[256,3584]{1,0:T(8,128)(2,1)}, u32[]{:S(2)}, u32[]{:S(2)}) collective-permute-start(bf16[256,3584]{1,0:T(8,128)(2,1)} %collective-permute-done), channel_id=1, source_target_pairs={{8,16},{12,20},{16,24},{20,28},{9,17},{13,21},{17,25},{21,29},{10,... | collective-permute-start | bytes 5505032 | tf_op jit(solution)/shard_map/ppermute | solution.py:90
  68.9 47.5 %collective-permute-start.4 = (bf16[256,3584]{1,0:T(8,128)(2,1)}, bf16[256,3584]{1,0:T(8,128)(2,1)}, u32[]{:S(2)}, u32[]{:S(2)}) collective-permute-start(bf16[256,3584]{1,0:T(8,128)(2,1)} %collective-permute-done.1), channel_id=1, source_target_pairs={{8,0},{12,4},{16,8},{20,12},{9,1},{13,5},{17,9},{21,13},{10,2},{14... | collective-permute-start | bytes 5505032 | tf_op jit(solution)/shard_map/ppermute | solution.py:93
  72.1 18.2 %copy-start.2 = (bf16[256,3584]{1,0:T(8,128)(2,1)}, bf16[256,3584]{1,0:T(8,128)(2,1)S(1)}, u32[]{:S(2)}) copy-start(bf16[256,3584]{1,0:T(8,128)(2,1)S(1)} %broadcast_select_fusion.refs_1_) | copy-start | bytes 5505028
  72.1 42.9 %collective-permute-start.5 = (bf16[256,3584]{1,0:T(8,128)(2,1)S(1)}, bf16[256,3584]{1,0:T(8,128)(2,1)}, u32[]{:S(2)}, u32[]{:S(2)}) collective-permute-start(bf16[256,3584]{1,0:T(8,128)(2,1)S(1)} %broadcast_select_fusion.refs_1_), channel_id=1, source_target_pairs={{0,4},{4,0},{8,12},{12,8},{16,20},{20,16},{24,28},{28,24},{1,5},{5... | collective-permute-start | bytes 5505032 | tf_op jit(solution)/shard_map/ppermute | solution.py:106
  108.0 8.4 %copy-start.9 = (bf16[64,8,512]{2,0,1:T(8,128)(2,1)}, bf16[64,8,512]{2,0,1:T(8,128)(2,1)S(1)}, u32[]{:S(2)}) copy-start(bf16[64,8,512]{2,0,1:T(8,128)(2,1)S(1)} %all-to-all-done) | copy-start | bytes 1572868
  118.1 25.1 %copy-start.6 = (bf16[256,3584]{1,0:T(8,128)(2,1)}, bf16[256,3584]{1,0:T(8,128)(2,1)S(1)}, u32[]{:S(2)}) copy-start(bf16[256,3584]{1,0:T(8,128)(2,1)S(1)} %select_select_fusion.1.refs_2_) | copy-start | bytes 5505028
  118.2 41.4 %collective-permute-start.8 = (bf16[256,3584]{1,0:T(8,128)(2,1)S(1)}, bf16[256,3584]{1,0:T(8,128)(2,1)}, u32[]{:S(2)}, u32[]{:S(2)}) collective-permute-start(bf16[256,3584]{1,0:T(8,128)(2,1)S(1)} %select_select_fusion.1.refs_2_), channel_id=1, source_target_pairs={{0,4},{4,0},{8,12},{12,8},{16,20},{20,16},{24,28},{28,24},{1,5},{5... | collective-permute-start | bytes 5505032 | tf_op jit(solution)/shard_map/ppermute | solution.py:106
  120.0 39.5 %collective-permute-start.6 = (bf16[256,3584]{1,0:T(8,128)(2,1)}, bf16[256,3584]{1,0:T(8,128)(2,1)}, u32[]{:S(2)}, u32[]{:S(2)}) collective-permute-start(bf16[256,3584]{1,0:T(8,128)(2,1)} %collective-permute-done.3), channel_id=1, source_target_pairs={{16,24},{20,28},{17,25},{21,29},{18,26},{22,30},{19,27},{23,31}} | collective-permute-start | bytes 5505032 | tf_op jit(solution)/shard_map/ppermute | solution.py:90
  121.9 43.1 %collective-permute-start.7 = (bf16[256,3584]{1,0:T(8,128)(2,1)}, bf16[256,3584]{1,0:T(8,128)(2,1)}, u32[]{:S(2)}, u32[]{:S(2)}) collective-permute-start(bf16[256,3584]{1,0:T(8,128)(2,1)} %collective-permute-done.4), channel_id=1, source_target_pairs={{8,0},{12,4},{9,1},{13,5},{10,2},{14,6},{11,3},{15,7}} | collective-permute-start | bytes 5505032 | tf_op jit(solution)/shard_map/ppermute | solution.py:93
  166.8 39.7 %collective-permute-start.9 = (bf16[256,3584]{1,0:T(8,128)(2,1)S(1)}, bf16[256,3584]{1,0:T(8,128)(2,1)}, u32[]{:S(2)}, u32[]{:S(2)}) collective-permute-start(bf16[256,3584]{1,0:T(8,128)(2,1)S(1)} %select_select_fusion.refs_3_), channel_id=1, source_target_pairs={{0,4},{4,0},{8,12},{12,8},{16,20},{20,16},{24,28},{28,24},{1,5},{5... | collective-permute-start | bytes 5505032 | tf_op jit(solution)/shard_map/ppermute | solution.py:106
  171.1 1.5 copy-start.3
  175.6 30.9 %copy-start.1 = (bf16[8,512,256]{2,1,0:T(8,128)(2,1)S(1)}, bf16[8,512,256]{2,1,0:T(8,128)(2,1)}, u32[]{:S(2)}) copy-start(bf16[8,512,256]{2,1,0:T(8,128)(2,1)} %copy.21.grad_ref) | copy-start | bytes 6291460
  206.5 3.1 %copy-start = (f32[512,3584]{1,0:T(8,128)S(1)}, f32[512,3584]{1,0:T(8,128)}, u32[]{:S(2)}) copy-start(f32[512,3584]{1,0:T(8,128)} %shard_map.101.master_ref) | copy-start | bytes 22020100
  (2 other events, 3.0 us)
Sparse Core Ops, SparseCore 0:
  9.6 25.2 all-gather.3
  58.8 47.0 reduce-scatter.1
  116.5 23.5 all-gather.5
